TPU v7x, 32 devices: a whole 2x2x4 slice. The times are simulated.
32 devices in a mesh: groups: 2 (over x), seq: 16 (over z, y, core).
Axes of the slice: x: 2, y: 2, z: 4, core: 2. Of those that a mesh axis runs over, the one named last changes fastest.
Arguments:
- query_raw: bfloat16 [4096, 2048], P(('groups', 'seq')), parts along dimension 0, may hold values from -6 to 6
- key_raw: bfloat16 [4096, 4096], P(('groups', 'seq')), parts along dimension 0, may hold values from -72 to 72
- value_raw: bfloat16 [4096, 4096], P(('groups', 'seq')), parts along dimension 0, may hold values from -6 to 6
- beta_raw: float32 [4096, 32], P(('groups', 'seq')), parts along dimension 0, may hold values from -6 to 1
- gate_raw: float32 [4096, 16], P(('groups', 'seq')), parts along dimension 0, may hold values from 0.3 to 10.6
- conv_weight: float32 [4, 10240], replicated, may hold values from -2.5 to 2.5
- out_grad: bfloat16 [4096, 2048], P(('groups', 'seq')), parts along dimension 0, may hold values from -6 to 6
Outputs:
- mixed: bfloat16 [4096, 2048], P(('groups', 'seq')), parts along dimension 0
- query_grad: bfloat16 [4096, 2048], P(('groups', 'seq')), parts along dimension 0
- key_grad: bfloat16 [4096, 4096], P(('groups', 'seq')), parts along dimension 0
- value_grad: bfloat16 [4096, 4096], P(('groups', 'seq')), parts along dimension 0
- beta_grad: float32 [4096, 32], P(('groups', 'seq')), parts along dimension 0
- gate_grad: float32 [4096, 16], P(('groups', 'seq')), parts along dimension 0
- conv_grad: float32 [8, 10240], P('groups'), parts along dimension 0
There are 2 independent parts, one for each index of `groups`. A program takes and returns all parts, laid end to end along the dimension named above; an argument that names none is the same for every part. Nothing has to cross between parts.
All inputs are finite; a program needn't handle non-finite values.
Results may differ from a plain program's by a relative error of at most 0.001.
Values may be sent and summed in bfloat16 or wider, within the bound.
A program may use at most 384 MiB of HBM per device.

v0:
```python
import math

import jax
import jax.numpy as jnp
from jax import lax
from jax.sharding import PartitionSpec as P

DK = 128
DV = 128


highest_precision = lax.Precision.HIGHEST


def shifted(x, axis, by):
    size = lax.axis_size(axis)
    pairs = [(i, i + by) for i in range(size) if 0 <= i + by < size]
    return lax.ppermute(x, axis, pairs)


def prefix_2(part, axis, combine, identity, reverse):
    count = lax.axis_size(axis)
    place = lax.axis_index(axis)
    ahead = count - 1 - place if reverse else place
    gathered = jax.tree.map(lambda a: lax.all_gather(a, axis), part)
    state = jax.tree.map(lambda a, e: jnp.zeros_like(a) + jnp.asarray(e, a.dtype), part, identity)

    def one(lap, state):
        source = count - 1 - lap if reverse else lap
        return combine(
            state, jax.tree.map(lambda a: lax.dynamic_index_in_dim(a, source, 0, False), gathered)
        )

    return lax.fori_loop(0, ahead, one, state)


def prepare_feats(extended, weights, beta_in, gate_in):
    tap_count = weights.shape[0]
    tok_rows = extended.shape[0] - tap_count + 1
    convolved = weights[0] * extended[0:tok_rows]
    for offset in range(1, tap_count):
        convolved = convolved + weights[offset] * extended[offset : offset + tok_rows]
    activated = jax.nn.silu(convolved)
    head_count = gate_in.shape[1]
    query_cols = head_count * DK
    queries = activated[:, :query_cols].reshape(tok_rows, head_count, DK).transpose(1, 0, 2)
    key_pre = activated[:, query_cols : 3 * query_cols].reshape(tok_rows, 2, head_count, DK)
    key_rows = key_pre / jnp.sqrt(jnp.sum(key_pre * key_pre, axis=-1, keepdims=True) + 1e-06)
    key_rows = key_rows.transpose(2, 0, 1, 3).reshape(head_count, 2 * tok_rows, DK)
    values = activated[:, 3 * query_cols :].reshape(tok_rows, 2, head_count, DV)
    values = values.transpose(2, 0, 1, 3).reshape(head_count, 2 * tok_rows, DV)
    beta_rows = (
        jax.nn.sigmoid(beta_in)
        .reshape(tok_rows, 2, head_count)
        .transpose(2, 0, 1)
        .reshape(head_count, 2 * tok_rows)
    )
    log_gate = jax.nn.log_sigmoid(gate_in)
    log_steps = (
        jnp.stack([log_gate, jnp.zeros_like(log_gate)], axis=1)
        .transpose(2, 0, 1)
        .reshape(head_count, 2 * tok_rows)
    )
    return (queries, key_rows, values, beta_rows, log_steps)


def block_tables(features):
    queries, key_rows, values, beta_rows, log_steps = features
    head_count, sub_total = beta_rows.shape
    key_size = key_rows.shape[-1]
    sub_len = math.gcd(sub_total, 128)
    pieces = sub_total // sub_len
    half_len = sub_len // 2
    key_blocks = key_rows.reshape(head_count, pieces, sub_len, key_size)
    value_blocks = values.reshape(head_count, pieces, sub_len, values.shape[-1])
    beta_blocks = beta_rows.reshape(head_count, pieces, sub_len)
    log_blocks = log_steps.reshape(head_count, pieces, sub_len)
    probe_segment_lines = queries.reshape(head_count, pieces, half_len, key_size)
    cumul = jnp.cumsum(log_blocks, axis=-1)
    positions = jnp.arange(sub_len)
    below_mask = positions[:, None] > positions[None, :]
    key_inner = jnp.einsum("hcid,hcjd->hcij", key_blocks, key_blocks, precision=highest_precision)
    gap_logs = jnp.where(below_mask, cumul[..., :, None] - cumul[..., None, :], 0.0)
    decay_low = jnp.where(below_mask, jnp.exp(gap_logs), 0.0)
    system = jnp.eye(sub_len, dtype=jnp.float32) + beta_blocks[..., :, None] * decay_low * key_inner
    right_side = jnp.concatenate(
        [
            (beta_blocks * jnp.exp(cumul))[..., None] * key_blocks,
            beta_blocks[..., None] * value_blocks,
        ],
        axis=-1,
    )
    solved = jax.scipy.linalg.solve_triangular(system, right_side, lower=True)
    w_table = solved[..., :key_size]
    base_values = solved[..., key_size:]
    last_log = cumul[..., -1:]
    scaled_keys = jnp.exp(last_log - cumul)[..., None] * key_blocks
    end_gain = jnp.exp(last_log[..., 0])
    odd_logs = cumul[..., 1::2]
    odd_rows = 2 * jnp.arange(half_len) + 1
    reach_mask = positions[None, :] <= odd_rows[:, None]
    query_key = jnp.einsum(
        "hcmd,hcjd->hcmj", probe_segment_lines, key_blocks, precision=highest_precision
    )
    out_logs = jnp.where(reach_mask, odd_logs[..., :, None] - cumul[..., None, :], 0.0)
    out_mix = jnp.where(reach_mask, jnp.exp(out_logs), 0.0) * query_key
    query_gain = jnp.exp(odd_logs)
    return tuple(
        (
            jnp.moveaxis(table_part, 1, 0)
            for table_part in (
                probe_segment_lines,
                out_mix,
                query_gain,
                w_table,
                base_values,
                scaled_keys,
                end_gain,
            )
        )
    )


def run_blocks(carry_state, tables):

    def block_step(current_block, block_row):
        probe_segment_lines, out_mix, query_gain, w_table, base_values, scaled_keys, end_gain = (
            block_row
        )
        update = base_values - jnp.einsum(
            "hcd,hvd->hcv", w_table, current_block, precision=highest_precision
        )
        out_block = query_gain[..., None] * jnp.einsum(
            "fwb,fib->fwi", probe_segment_lines, current_block, precision=highest_precision
        )
        out_block = out_block + jnp.einsum(
            "hmc,hcv->hmv", out_mix, update, precision=highest_precision
        )
        current_block = end_gain[:, None, None] * current_block + jnp.einsum(
            "hcv,hcd->hvd", update, scaled_keys, precision=highest_precision
        )
        return (current_block, out_block)

    final_state, out_blocks = lax.scan(block_step, carry_state, tables)
    pieces, head_count, half_len, value_size = out_blocks.shape
    mixed_out = out_blocks.transpose(0, 2, 1, 3).reshape(pieces * half_len, head_count * value_size)
    return (mixed_out, final_state)


def device_map(tables):
    head_count = tables[3].shape[1]

    def map_step(carry_maps, block_row):
        mat_part, off_part = carry_maps
        w_table, base_values, scaled_keys, end_gain = block_row
        mat_next = end_gain[:, None, None] * mat_part - jnp.einsum(
            "hkc,hcd->hkd",
            jnp.einsum("hkj,hcj->hkc", mat_part, w_table, precision=highest_precision),
            scaled_keys,
            precision=highest_precision,
        )
        update = base_values - jnp.einsum(
            "hcd,hvd->hcv", w_table, off_part, precision=highest_precision
        )
        off_next = end_gain[:, None, None] * off_part + jnp.einsum(
            "hcv,hcd->hvd", update, scaled_keys, precision=highest_precision
        )
        return ((mat_next, off_next), None)

    start_maps = (
        jnp.broadcast_to(jnp.eye(DK, dtype=jnp.float32), (head_count, DK, DK)),
        jnp.zeros((head_count, DV, DK), jnp.float32),
    )
    final_maps, _ = lax.scan(map_step, start_maps, (tables[3], tables[4], tables[5], tables[6]))
    return final_maps


def compose_maps(earlier, later):
    mat_first, off_first = earlier
    mat_second, off_second = later
    mat_joint = jnp.einsum("hij,hjk->hik", mat_first, mat_second, precision=highest_precision)
    off_joint = (
        jnp.einsum("hij,hjk->hik", off_first, mat_second, precision=highest_precision) + off_second
    )
    return (mat_joint, off_joint)


def body(query_raw, key_raw, value_raw, beta_raw, gate_raw, conv_weight, out_grad):
    tok_rows = query_raw.shape[0]
    margin = conv_weight.shape[0] - 1
    joined = jnp.concatenate([query_raw, key_raw, value_raw], axis=1)
    earlier_rows = shifted(joined[tok_rows - margin :], "seq", 1)
    extended = jnp.concatenate([earlier_rows, joined], axis=0).astype(jnp.float32)
    features, prep_back = jax.vjp(prepare_feats, extended, conv_weight, beta_raw, gate_raw)
    tables, table_back = jax.vjp(block_tables, features)
    out_cot = out_grad.astype(jnp.float32)
    mat_map, off_map = device_map(tables)
    identity = (
        jnp.broadcast_to(jnp.eye(DK, dtype=jnp.float32), mat_map.shape),
        jnp.zeros_like(off_map),
    )
    prefix = prefix_2((mat_map, off_map), "seq", compose_maps, identity, False)
    state_in = prefix[1]

    def outputs_only(carry_state):
        return run_blocks(carry_state, tables)[0]

    _, state_back = jax.vjp(outputs_only, state_in)
    local_grad = state_back(out_cot)[0]
    suffix = prefix_2(
        (jnp.swapaxes(mat_map, 1, 2), local_grad), "seq", compose_maps, identity, True
    )
    carry_grad = suffix[1]
    (mixed_out, final_state), reverse_sweep = jax.vjp(run_blocks, state_in, tables)
    grad_start, grad_tables = reverse_sweep((out_cot, carry_grad))
    feature_cotangents = table_back(grad_tables)[0]
    grad_ext, grad_conv, grad_beta, grad_gate = prep_back(feature_cotangents)
    later_grads = shifted(grad_ext[:margin], "seq", -1)
    grad_joined = grad_ext[margin:].at[tok_rows - margin :].add(later_grads)
    conv_total = lax.psum(grad_conv, "seq")
    query_cols = query_raw.shape[1]
    key_cols = key_raw.shape[1]
    return (
        mixed_out.astype(jnp.bfloat16),
        grad_joined[:, :query_cols].astype(jnp.bfloat16),
        grad_joined[:, query_cols : query_cols + key_cols].astype(jnp.bfloat16),
        grad_joined[:, query_cols + key_cols :].astype(jnp.bfloat16),
        grad_beta,
        grad_gate,
        conv_total,
    )


def solution(mesh):
    in_specs = (
        P(("groups", "seq"), None),
        P(("groups", "seq"), None),
        P(("groups", "seq"), None),
        P(("groups", "seq"), None),
        P(("groups", "seq"), None),
        P(),
        P(("groups", "seq"), None),
    )
    out_specs = (
        P(("groups", "seq"), None),
        P(("groups", "seq"), None),
        P(("groups", "seq"), None),
        P(("groups", "seq"), None),
        P(("groups", "seq"), None),
        P(("groups", "seq"), None),
        P("groups", None),
    )
    return jax.shard_map(body, mesh=mesh, in_specs=in_specs, out_specs=out_specs, check_vma=False)
```

profile of v0, /device:TPU:8, one launch (start us, length us, event | category | flops | bytes accessed | tf_op | source)
XLA Modules:
  0.0 1276.0 jit_solution(6922559796064815109)
XLA Ops:
  18.8 4.6 fusion.110
  31.4 4.5 fusion.188
  40.2 315.8 %custom-call.10 = f32[16,2,1,128,128]{3,4,2,1,0:T(8,128)} custom-call(f32[16,2,1,128,128]{4,3,2,1,0:T(8,128)} %get-tuple-element.1497), custom_call_target="InvertDiagBlocksLowerTriangular" | custom-call | tf_op jit(solution)/shard_map/jvp(jit(_solve_triangular))/vmap(vmap())/triangular_solve | solution.py:93
  358.3 3.8 fusion.111
  366.8 5.1 bitcast_multiply_fusion.12
  376.1 21.3 %while.123 = (s32[]{:T(128)}, f32[16,128,128]{2,1,0:T(8,128)}, f32[2,16,1,1]{1,3,2,0:T(1,128)S(1)}, f32[2,16,64,1]{2,1,3,0:T(8,128)S(1)}, f32[2,16,64,128]{3,2,1...) while((s32[]{:T(128)}, f32[16,128,128]{2,1,0:T(8,128)}, ...), condition=%wide.region_11.12_spmd.clone, body=%wide.region_10.11_spmd.clone.sunk | while | flops 1209925632 | bytes 30428520 | solution.py:144
  376.3 3.2 convolution_add_fusion.20
  386.7 3.6 convolution_add_fusion.20
  397.4 3.4 copy.424
  401.9 23.9 %while.122 = (s32[]{:T(128)}, f32[16,128,128]{2,1,0:T(8,128)}, f32[16,128,128]{2,1,0:T(8,128)}, f32[2,16]{1,0:T(2,128)S(1)}, f32[2,16,128,128]{3,2,1,0:T(8,128)S...) while((s32[]{:T(128)}, f32[16,128,128]{2,1,0:T(8,128)}, ...), condition=%wide.region_3.4_spmd.clone, body=%wide.region_2.3_spmd.clone.sunk | while | flops 1612447744 | bytes 40896896 | solution.py:174
  402.3 3.7 convolution_subtract_fusion.6
  414.0 4.0 convolution_subtract_fusion.6
  425.9 3.3 copy.440
  430.8 93.0 %all-gather.15.cloned.1.call-done = f32[256,128,128]{2,1,0:T(8,128)} async-done(((f32[16,128,128]{2,1,0:T(8,128)}), f32[256,128,128]{2,1,0:T(8,128)}) %all-gather.15.cloned.1.call-update) | async-done | bytes 16777232 | tf_op jit(solution)/shard_map/all_gather | solution.py:25
  523.9 127.3 %all-gather.13.cloned.1.call-done = f32[256,128,128]{2,1,0:T(8,128)} async-done(((f32[16,128,128]{2,1,0:T(8,128)}), f32[256,128,128]{2,1,0:T(8,128)}) %all-gather.13.cloned.1.call-update) | async-done | bytes 16777232 | tf_op jit(solution)/shard_map/all_gather | solution.py:25
  651.2 53.8 %while.120 = (s32[]{:T(128)}, f32[16,128,128]{1,2,0:T(8,128)S(1)}, s32[]{:T(128)}, f32[16,16,128,128]{3,2,1,0:T(8,128)}, f32[16,16,128,128]{3,2,1,0:T(8,128)}, /*index=5*/s32[]{:T(128)}, s32[]{:T(128)}, s32[]{:T(128)}, s32[]{:T(128)}) while((s32[]{:T(128)}, f32[16,128,128]{1,2,0:T(8,128)S(1)}, s32[]{:T(128)}, ...), condition=%wide.region_13.14_spmd, body=%wide.region_12.13_spmd.sunk | while | flops 402915328 | bytes 10485907 | solution.py:34
  657.8 3.1 fusion.278
  662.8 3.2 fusion.278
  677.5 3.1 fusion.278
  682.4 3.1 fusion.278
  697.1 3.1 fusion.278
  705.4 73.5 %all-gather.9.cloned.1.call-done = f32[256,128,128]{2,1,0:T(8,128)} async-done(((f32[16,128,128]{2,1,0:T(8,128)}), f32[256,128,128]{2,1,0:T(8,128)}) %all-gather.9.cloned.1.call-update) | async-done | bytes 16777232 | tf_op jit(solution)/shard_map/all_gather | solution.py:25
  779.0 127.7 %all-gather.11.cloned.1.call-done = f32[256,128,128]{2,1,0:T(8,128)} async-done(((f32[16,128,128]{2,1,0:T(8,128)}), f32[256,128,128]{2,1,0:T(8,128)}) %all-gather.11.cloned.1.call-update) | async-done | bytes 16777232 | tf_op jit(solution)/shard_map/all_gather | solution.py:25
  907.7 28.0 %while.117 = (s32[]{:T(128)}, f32[16,128,128]{1,2,0:T(8,128)}, s32[]{:T(128)}, f32[16,16,128,128]{3,2,1,0:T(8,128)}, f32[16,16,128,128]{3,2,1,0:T(8,128)}, /*index=5*/s32[]{:T(128)}, s32[]{:T(128)}, s32[]{:T(128)}) while((s32[]{:T(128)}, f32[16,128,128]{1,2,0:T(8,128)}, s32[]{:T(128)}, f32[16,16,128,128]{3,2,1,0:T(8,128)}, ...), condition=%wide.region_5.6_spmd, body=%wide.region_4.5_spmd.sunk | while | flops 402915328 | bytes 10485887 | solution.py:34
  910.6 4.1 fusion.267
  917.5 4.1 fusion.267
  924.5 4.1 fusion.267
  931.5 4.1 fusion.267
  940.5 26.2 %while.118 = (s32[]{:T(128)}, f32[16,128,128]{2,1,0:T(8,128)S(1)}, bf16[2,16,64,128]{3,2,1,0:T(8,128)(2,1)}, f32[2,16,128,128]{3,2,1,0:T(8,128)}, f32[2,16,64,12...) while((s32[]{:T(128)}, f32[16,128,128]{2,1,0:T(8,128)S(1)}, ...), condition=%wide.region_7.8_spmd, body=%wide.region_6.7_spmd.sunk | while | flops 1209008128 | bytes 58758156 | solution.py:144
  940.5 5.0 bitcast_dynamic-update-slice_fusion.12
  953.6 4.9 bitcast_dynamic-update-slice_fusion.12
  973.6 43.5 %while.121 = (s32[]{:T(128)}, f32[16,128,128]{2,1,0:T(8,128)S(1)}, f32[2,16,64,128]{3,2,0,1:T(8,128)}, f32[2,16,64,128]{3,2,0,1:T(8,128)}, f32[2,16,64]{2,1,0:T(...) while((s32[]{:T(128)}, f32[16,128,128]{2,1,0:T(8,128)S(1)}, ...), condition=%wide.region_17.18_spmd, body=%wide.region_14.17_spmd.sunk | while | flops 2418539520 | bytes 108052928 | solution.py:144
  973.8 3.4 convolution_add_fusion.17
  990.9 4.3 fusion.294
  995.2 3.4 convolution_add_fusion.17
  1012.3 4.3 fusion.294
  1017.7 7.9 fusion.115
  1025.6 5.6 fusion.117
  1031.3 7.9 multiply_reduce_fusion.5
  1039.2 4.7 fusion.137
  1043.9 3.8 fusion.154
  1047.7 3.9 fusion.124
  1056.6 3.6 add_add_fusion
  1071.3 8.2 multiply_reduce_fusion.3
  1079.5 10.3 broadcast_multiply_fusion
  1097.2 3.3 pad_add_fusion
  1113.2 3.5 collective-permute-done.1
  1121.7 145.8 %all-reduce.18.cloned.1.call-done = f32[4,10240]{1,0:T(4,128)} async-done(((f32[4,10240]{1,0:T(4,128)}), f32[4,10240]{1,0:T(4,128)}) %all-reduce.18.cloned.1.call-update) | async-done | bytes 163856 | tf_op jit(solution)/shard_map/psum | solution.py:220
  (546 shorter events, 215.1 us)
Async XLA Ops:
  7.2 516.7 %all-gather.15.cloned.1.call-start = ((), (), s32[]{:S(2)}) async-start(), calls=%async_computation.4 | async-start | bytes 17825792 | tf_op jit(solution)/shard_map/all_gather | solution.py:25
  8.4 4.9 copy-start.119
  9.7 4.7 copy-start.108
  9.7 5.4 copy-start.98
  9.7 6.0 copy-start.73
  11.4 6.7 collective-permute-start
  14.3 23.1 %copy-start.64 = (f32[16,2,128]{2,1,0:T(2,128)}, f32[16,2,128]{2,1,0:T(2,128)S(1)}, u32[]{:S(2)}) copy-start(f32[16,2,128]{2,1,0:T(2,128)S(1)} %copy.411) | copy-start | bytes 49156
  14.7 22.7 %copy-start.89 = (f32[16,2,128]{2,1,0:T(2,128)}, f32[16,2,128]{2,1,0:T(2,128)S(1)}, u32[]{:S(2)}) copy-start(f32[16,2,128]{2,1,0:T(2,128)S(1)} %copy.410) | copy-start | bytes 49156
  15.1 415.5 %copy-start.77 = (f32[16,2,64]{2,0,1:T(8,128)}, f32[16,2,64]{2,0,1:T(8,128)S(1)}, u32[]{:S(2)}) copy-start(f32[16,2,64]{2,0,1:T(8,128)S(1)} %slice.118) | copy-start | bytes 24580
  15.4 340.6 %copy-start.102 = (f32[16,2,128]{2,1,0:T(2,128)}, f32[16,2,128]{2,1,0:T(2,128)S(1)}, u32[]{:S(2)}) copy-start(f32[16,2,128]{2,1,0:T(2,128)S(1)} %copy.418) | copy-start | bytes 49156
  15.4 340.6 %copy-start.104 = (f32[16,2,128]{2,1,0:T(2,128)}, f32[16,2,128]{2,1,0:T(2,128)S(1)}, u32[]{:S(2)}) copy-start(f32[16,2,128]{2,1,0:T(2,128)S(1)} %copy.421) | copy-start | bytes 49156
  15.6 350.6 %copy-start.95 = (pred[64,128]{1,0:T(8,128)(4,1)}, pred[64,128]{1,0:T(8,128)(4,1)S(1)}, u32[]{:S(2)}) copy-start(pred[64,128]{1,0:T(8,128)(4,1)S(1)} %iota_compare_fusion.3) | copy-start | bytes 24580
  16.5 20.9 %copy-start.91 = (pred[128,128]{1,0:T(8,128)(4,1)}, pred[128,128]{1,0:T(8,128)(4,1)S(1)}, u32[]{:S(2)}) copy-start(pred[128,128]{1,0:T(8,128)(4,1)S(1)} %get-tuple-element.1504) | copy-start | bytes 49156
  16.5 20.9 %copy-start.93 = (pred[128,128]{1,0:T(8,128)(4,1)}, pred[128,128]{1,0:T(8,128)(4,1)S(1)}, u32[]{:S(2)}) copy-start(pred[128,128]{1,0:T(8,128)(4,1)S(1)} %get-tuple-element.1505) | copy-start | bytes 49156
  31.4 324.6 %copy-start.14 = (f32[16,128,2,128]{3,2,1,0:T(2,128)}, f32[16,128,2,128]{3,2,1,0:T(2,128)S(1)}, u32[]{:S(2)}) copy-start(f32[16,128,2,128]{3,2,1,0:T(2,128)S(1)} %copy.415) | copy-start | bytes 6291460
  366.2 5.8 copy-start.47
  397.4 253.7 %all-gather.13.cloned.1.call-start = ((), (), s32[]{:S(2)}) async-start(), calls=%async_computation.3 | async-start | bytes 17825792 | tf_op jit(solution)/shard_map/all_gather | solution.py:25
  429.2 349.7 %all-gather.9.cloned.1.call-start = ((), (), s32[]{:S(2)}) async-start(), calls=%async_computation.1 | async-start | bytes 17825792 | tf_op jit(solution)/shard_map/all_gather | solution.py:25
  430.0 476.7 %all-gather.11.cloned.1.call-start = ((), (), s32[]{:S(2)}) async-start(), calls=%async_computation.2 | async-start | bytes 17825792 | tf_op jit(solution)/shard_map/all_gather | solution.py:25
  430.5 836.9 %all-reduce.18.cloned.1.call-start = ((), (), s32[]{:S(2)}) async-start(), calls=%async_computation | async-start | bytes 327680 | tf_op jit(solution)/shard_map/psum | solution.py:220
  430.6 613.2 %copy-start.87 = (f32[16,2,64]{2,1,0:T(2,128)}, f32[16,2,64]{2,1,0:T(2,128)S(1)}, u32[]{:S(2)}) copy-start(f32[16,2,64]{2,1,0:T(2,128)S(1)} %copy.459) | copy-start | bytes 24580
  940.5 5.0 copy-start.28
  940.5 5.0 copy-start.53
  953.6 5.0 copy-start.28
  953.6 5.0 copy-start.53
  1017.6 7.9 copy-start.35
  1017.7 7.9 copy-start.38
  1025.5 5.7 copy-start.16
  1025.6 5.7 copy-start.40
  1025.6 5.7 copy-start.42
  1025.6 5.7 copy-start.45
  1025.6 5.7 copy-start.65
  1025.6 5.7 copy-start.90
  1025.6 5.7 copy-start.92
  1025.6 5.7 copy-start.94
  1039.2 4.7 copy-start.96
  1047.7 5.3 copy-start.31
  1063.2 6.6 slice-start
  1064.4 5.4 slice-start.1
  1071.3 8.2 copy-start.80
  1071.3 8.2 copy-start.82
  1071.3 8.2 copy-start.84
  1071.3 8.2 copy-start.86
  1089.8 5.8 copy-start.23
  1089.8 7.3 copy-start.24
  1100.5 5.2 copy-start.72
  1106.6 10.1 collective-permute-start.1
  1108.7 8.1 copy-start.21
  (111 other events, 290.6 us)
Sparse Core Ops, SparseCore 0:
  397.5 126.3 all-gather.14
  526.0 125.0 all-gather.12
  653.9 125.0 all-gather.8
  781.5 125.0 all-gather.10
  1101.5 165.9 all-reduce.17
where the time goes:
time: 1290 us; the launch traced here: 1280 us
  waiting for transfers between devices  574 us (44%)
  other arithmetic  366 us (28%)
  matrix products  198 us (15%)
  local copies, waits for them, and re-layouts  116 us (9%)
  between operations  15.8 us (1%)
    all_gather x4, waiting for transfers between devices, prefix_2(): gathered = jax.tree.map(lambda a: lax.all_gather(a, axis), part)  422 us
    another operation x2, other arithmetic, block_tables(): solved = jax.scipy.linalg.solve_triangular(system, right_side, lower=True)  319 us
    psum x1, waiting for transfers between devices, body(): conv_total = lax.psum(grad_conv, 'seq')  146 us
    dot_general x15, matrix products, compose_maps(): jnp.einsum('hij,hjk->hik', off_first, mat_second, precision=highest_preci...  50.7 us
    unnamed x210, local copies, waits for them, and re-layouts  35.6 us
  transfers between devices with their start and end apart: 7, of which 7 were waited for; matrix products, arithmetic and copies ran while one was open for 8% of the time, Pallas kernels for 0%

commit v1 on v0

v1 whole, which is shorter than its diff:
```python
import jax
import jax.numpy as jnp
from jax import lax
from jax.sharding import PartitionSpec as P

DK = 128
DV = 128

HIGH = lax.Precision.HIGH
HIGHEST = lax.Precision.HIGHEST


def mm(spec, a, b, precision=HIGH):
    return jnp.einsum(spec, a, b, precision=precision, preferred_element_type=jnp.float32)


def shifted(x, axis, by):
    size = lax.axis_size(axis)
    pairs = [(i, i + by) for i in range(size) if 0 <= i + by < size]
    return lax.ppermute(x, axis, pairs)


def order_of(count):
    index = jnp.arange(count)
    half = count // 2
    return 2 * (index % half) + index // half


def inverse(system):
    count = system.shape[-1]
    place = order_of(count)
    rows, cols = place[:, None], place[None, :]

    def corner(size):
        mask = (rows // (2 * size) == cols // (2 * size)) & (rows // size > cols // size)
        return jnp.where(mask, system, 0.0)

    found = jnp.eye(count, dtype=jnp.float32) - corner(1)
    size = 2
    while size < count:
        found = found - mm("hij,hjk->hik", found, mm("hij,hjk->hik", corner(size), found))
        size *= 2
    return found


@jax.custom_vjp
def solve(system, right):
    return mm("hij,hjk->hik", inverse(system), right)


def solve_fwd(system, right):
    inv = inverse(system)
    out = mm("hij,hjk->hik", inv, right)
    return out, (inv, out)


def solve_bwd(saved, cot):
    inv, out = saved
    right_cot = mm("hji,hjk->hik", inv, cot)
    return -mm("hik,hjk->hij", right_cot, out), right_cot


solve.defvjp(solve_fwd, solve_bwd)


def prepare_feats(extended, weights, beta_in, gate_in):
    tap_count = weights.shape[0]
    tok_rows = extended.shape[0] - tap_count + 1
    convolved = weights[0] * extended[0:tok_rows]
    for offset in range(1, tap_count):
        convolved = convolved + weights[offset] * extended[offset : offset + tok_rows]
    activated = jax.nn.silu(convolved)
    heads = gate_in.shape[1]
    query_cols = heads * DK
    queries = activated[:, :query_cols].reshape(tok_rows, heads, DK).transpose(1, 0, 2)
    key_pre = activated[:, query_cols : 3 * query_cols].reshape(tok_rows, 2, heads, DK)
    key_rows = key_pre / jnp.sqrt(jnp.sum(key_pre * key_pre, axis=-1, keepdims=True) + 1e-06)
    key_rows = key_rows.transpose(2, 1, 0, 3).reshape(heads, 2 * tok_rows, DK)
    values = activated[:, 3 * query_cols :].reshape(tok_rows, 2, heads, DV)
    values = values.transpose(2, 1, 0, 3).reshape(heads, 2 * tok_rows, DV)
    betas = jax.nn.sigmoid(beta_in).reshape(tok_rows, 2, heads)
    betas = betas.transpose(2, 1, 0).reshape(heads, 2 * tok_rows)
    upto = jnp.tril(jnp.ones((tok_rows, tok_rows), jnp.float32))
    cumul = mm("th,st->hs", jax.nn.log_sigmoid(gate_in), upto, HIGHEST)
    return queries, key_rows, values, betas, cumul


def chunk_tables(features):
    queries, keys, values, betas, cumul_tok = features
    count = keys.shape[1]
    place = order_of(count)
    cumul = jnp.concatenate([cumul_tok, cumul_tok], axis=1)
    below = place[:, None] > place[None, :]
    gaps = jnp.where(below, cumul[:, :, None] - cumul[:, None, :], 0.0)
    decay = jnp.where(below, jnp.exp(gaps), 0.0)
    inner = mm("hid,hjd->hij", keys, keys)
    system = jnp.eye(count, dtype=jnp.float32) + betas[:, :, None] * decay * inner
    right = jnp.concatenate(
        [(betas * jnp.exp(cumul))[..., None] * keys, betas[..., None] * values], axis=-1
    )
    solved = solve(system, right)
    w_table, base = solved[..., :DK], solved[..., DK:]
    last = cumul_tok[:, -1:]
    scaled_keys = jnp.exp(last - cumul)[..., None] * keys
    end_gain = jnp.exp(last[:, 0])
    half = count // 2
    reach = place[None, :] <= 2 * jnp.arange(half)[:, None] + 1
    out_logs = jnp.where(reach, cumul_tok[:, :, None] - cumul[:, None, :], 0.0)
    out_mix = jnp.where(reach, jnp.exp(out_logs), 0.0) * mm("hmd,hjd->hmj", queries, keys)
    probe = jnp.exp(cumul_tok)[..., None] * queries
    return probe, out_mix, w_table, base, scaled_keys, end_gain


def run_chunk(state, tables):
    probe, out_mix, w_table, base, scaled_keys, end_gain = tables
    update = base - mm("hcd,hvd->hcv", w_table, state)
    out = mm("hmd,hvd->hmv", probe, state) + mm("hmc,hcv->hmv", out_mix, update)
    final = end_gain[:, None, None] * state + mm("hcv,hcd->hvd", update, scaled_keys)
    return out, final


def chain(mats, offs, grads, axis):
    size = lax.axis_size(axis)
    heads = mats.shape[0]
    parts = max(1, size // heads)
    rows = DV // parts

    def spread(x):
        x = x.reshape((size, heads * parts // size) + x.shape[1:])
        return lax.all_to_all(x, axis, 0, 0)

    def cut(x):
        return x.reshape(heads * parts, rows, DK)

    mats = jnp.repeat(mats, parts, axis=0)
    packed = spread(jnp.concatenate([mats, cut(offs), cut(grads)], axis=1))
    mats, offs, grads = (
        packed[:, :, :DK],
        packed[:, :, DK : DK + rows],
        packed[:, :, DK + rows :],
    )
    states = [jnp.zeros_like(offs[0])]
    for i in range(size - 1):
        states.append(mm("hvk,hkd->hvd", states[-1], mats[i]) + offs[i])
    cots = [jnp.zeros_like(grads[0])]
    for i in range(size - 1, 0, -1):
        cots.append(mm("hvd,hkd->hvk", cots[-1], mats[i]) + grads[i])
    both = jnp.concatenate([jnp.stack(states), jnp.stack(cots[::-1])], axis=2)
    both = lax.all_to_all(both, axis, 0, 0).reshape(heads * parts, 2 * rows, DK)
    return (
        both[:, :rows].reshape(heads, DV, DK),
        both[:, rows:].reshape(heads, DV, DK),
    )


def body(query_raw, key_raw, value_raw, beta_raw, gate_raw, conv_weight, out_grad):
    tok_rows = query_raw.shape[0]
    heads = gate_raw.shape[1]
    margin = conv_weight.shape[0] - 1
    joined = jnp.concatenate([query_raw, key_raw, value_raw], axis=1)
    earlier_rows = shifted(joined[tok_rows - margin :], "seq", 1)
    extended = jnp.concatenate([earlier_rows, joined], axis=0).astype(jnp.float32)
    features, prep_back = jax.vjp(prepare_feats, extended, conv_weight, beta_raw, gate_raw)
    tables, table_back = jax.vjp(chunk_tables, features)
    probe, out_mix, w_table, base, scaled_keys, end_gain = tables
    out_cot = out_grad.astype(jnp.float32).reshape(tok_rows, heads, DV).transpose(1, 0, 2)
    mats = end_gain[:, None, None] * jnp.eye(DK, dtype=jnp.float32) - mm(
        "hck,hcd->hkd", w_table, scaled_keys
    )
    offs = mm("hcv,hcd->hvd", base, scaled_keys)
    mixed_cot = mm("hmv,hmc->hcv", out_cot, out_mix)
    grads = mm("hmv,hmd->hvd", out_cot, probe) - mm("hcv,hcd->hvd", mixed_cot, w_table)
    state_in, carry_grad = chain(mats, offs, grads, "seq")
    (out, _), run_back = jax.vjp(run_chunk, state_in, tables)
    _, table_cots = run_back((out_cot, carry_grad))
    grad_ext, grad_conv, grad_beta, grad_gate = prep_back(table_back(table_cots)[0])
    later_grads = shifted(grad_ext[:margin], "seq", -1)
    grad_joined = grad_ext[margin:].at[tok_rows - margin :].add(later_grads)
    conv_total = lax.psum(grad_conv, "seq")
    mixed = out.transpose(1, 0, 2).reshape(tok_rows, heads * DV)
    query_cols = query_raw.shape[1]
    key_cols = key_raw.shape[1]
    return (
        mixed.astype(jnp.bfloat16),
        grad_joined[:, :query_cols].astype(jnp.bfloat16),
        grad_joined[:, query_cols : query_cols + key_cols].astype(jnp.bfloat16),
        grad_joined[:, query_cols + key_cols :].astype(jnp.bfloat16),
        grad_beta,
        grad_gate,
        conv_total,
    )


def solution(mesh):
    rows = P(("groups", "seq"), None)
    return jax.shard_map(
        body,
        mesh=mesh,
        in_specs=(rows, rows, rows, rows, rows, P(), rows),
        out_specs=(rows, rows, rows, rows, rows, rows, P("groups", None)),
        check_vma=False,
    )
```

time: 1290 us -> 536 us (0.42)
  waiting for transfers between devices: 574 us -> 135 us
  other arithmetic: 366 us -> 96.6 us
  matrix products: 198 us -> 167 us
  local copies, waits for them, and re-layouts: 116 us -> 95.1 us
  starting transfers between devices: 4.18 us -> 17.3 us
    all_gather x4 -> x0, waiting for transfers between devices: 422 us -> none  [prefix_2(): gathered = jax.tree.map(lambda a: lax.all_gather(a, axis), part)]
    another operation x7 -> x1, other arithmetic: 322 us -> 1.07 us  [the longest x2 319 us: block_tables(): solved = jax.scipy.linalg.solve_triangular(system, right_side, lower=True)]
    psum x1, waiting for transfers between devices: 146 us -> 21.2 us  [body(): conv_total = lax.psum(grad_conv, 'seq')]
    all_to_all x0 -> x2, waiting for transfers between devices: none -> 113 us  [the longest x1 67.7 us: spread(): return lax.all_to_all(x, axis, 0, 0)]
    while x132 -> x0, local copies, waits for them, and re-layouts: 27 us -> none
    scatter-add x1, local copies, waits for them, and re-layouts: 1.47 us -> 27.4 us  [body(): grad_joined = grad_ext[margin:].at[tok_rows - margin:].add(later_grads)]
    dynamic_slice x32 -> x0, local copies, waits for them, and re-layouts: 24.6 us -> none  [the longest x30 24.6 us: one(): lax.dynamic_index_in_dim(a, source, 0, False)]
    another operation x3 -> x0, matrix products: 17.3 us -> none  [block_tables(): solved = jax.scipy.linalg.solve_triangular(system, right_side, lower=True)]
  transfers between devices with their start and end apart: 7 -> 5, of which waited for: 7 -> 3; matrix products, arithmetic and copies ran while one was open for 8% -> 14% of each run, Pallas kernels for 0% -> 0%
where the time goes in v1:
time: 536 us; the launch traced here: 527 us
  matrix products  167 us (31%)
  waiting for transfers between devices  135 us (25%)
  other arithmetic  96.6 us (18%)
  local copies, waits for them, and re-layouts  95.1 us (18%)
  starting transfers between devices  17.3 us (3%)
  between operations  15.8 us (3%)
    dot_general x64, matrix products, mm(): jnp.einsum(spec, a, b, precision=precision, preferred_element_type=jnp.fl...  160 us
    all_to_all x1, waiting for transfers between devices, spread(): return lax.all_to_all(x, axis, 0, 0)  67.7 us
    all_to_all x1, waiting for transfers between devices, chain(): both = lax.all_to_all(both, axis, 0, 0).reshape(heads * parts, 2 * rows, DK)  45.8 us
    scatter-add x1, local copies, waits for them, and re-layouts, body(): grad_joined = grad_ext[margin:].at[tok_rows - margin:].add(later_grads)  27.4 us
    unnamed x165, local copies, waits for them, and re-layouts  22 us
    reduce_sum x1, other arithmetic, prepare_feats(): convolved = convolved + weights[offset] * extended[offset:offset + tok_rows]  21.6 us
    psum x1, waiting for transfers between devices, body(): conv_total = lax.psum(grad_conv, 'seq')  21.2 us
    mul x1, other arithmetic, prepare_feats(): activated = jax.nn.silu(convolved)  11.9 us
  transfers between devices with their start and end apart: 5, of which 3 were waited for; matrix products, arithmetic and copies ran while one was open for 14% of the time, Pallas kernels for 0%

profile of v1, /device:TPU:8, one launch (start us, length us, event | category | flops | bytes accessed | tf_op | source)
XLA Modules:
  0.0 526.7 jit_solution(5668886342293127424)
XLA Ops:
  12.8 4.5 pad_maximum_fusion
  31.1 6.8 %maximum_convert_fusion = f32[131,10240]{0,1:T(8,128)S(1)} fusion(bf16[128,4096]{0,1:T(8,128)(2,1)} %copy.309, bf16[128,4096]{0,1:T(8,128)(2,1)} %copy.308, bf16[128,2048]{0,1:T(8,128)(2,1)} %copy.307, bf16[3,10240]{0,1:T(8,128)(2,1)S(1)} %copy.311), kind=kLoop, calls=%fused_computation.5 | loop fusion | flops 10731520 | bytes 8048640 | tf_op jit(solution)/shard_map/convert_element_type | solution.py:162
  38.0 11.9 %fusion.2 = (f32[128,10240]{0,1:T(8,128)S(1)}, f32[128,10240]{0,1:T(8,128)}) fusion(f32[131,10240]{0,1:T(8,128)S(1)} %maximum_convert_fusion, f32[10240]{0:T(1024)S(1)} %bitcast.509, f32[10240]{0:T(1024)S(1)} %bitcast.511, f32[10240]{0:T(1024)S(1)} %bitcast.507, f32[10240]{0:T(1024)S(1)} %bitcast.505), kind=kLoop, calls=%fused_computation.11 | loop fusion | flops 14417920 | bytes 31621120 | tf_op jit(solution)/shard_map/jvp(jit(silu))/mul | solution.py:72
  59.4 6.4 %fusion.23 = f32[16,256,256]{2,1,0:T(8,128)S(1)} fusion(f32[256,256]{0,1:T(8,128)S(1)} %copy-done.46, pred[256,256]{0,1:T(8,128)(4,1)S(1)} %copy-done.67, pred[256,256]{0,1:T(8,128)(4,1)S(1)} %copy-done.66, f32[16,256,256]{1,2,0:T(8,128)S(1)} %fusion.216, f32[16,256]{1,0:T(8,128)S(1)} %get-tuple-element.91, f32[16,256]{1,0:T(8,128)S(1)} %copy-done.49, ...), kind=kOutput, calls=%fused_computation.35 | convolution fusion | flops 1626341376 | bytes 8880128 | tf_op jit(solution)/shard_map/jvp(hij,hjk->hik)/dot_general | solution.py:14
  65.8 6.9 %fusion.25 = f32[16,256,256]{1,2,0:T(8,128)S(1)} fusion(f32[16,256,256]{2,1,0:T(8,128)S(1)} %fusion.23, f32[256,256]{0,1:T(8,128)S(1)} %copy-done.46, pred[256,256]{0,1:T(8,128)(4,1)S(1)} %copy-done.66, f32[16,256,256]{1,2,0:T(8,128)S(1)} %fusion.216, f32[16,256]{1,0:T(8,128)S(1)} %get-tuple-element.91, pred[256,256]{0,1:T(8,128)(4,1)S(1)} %copy-done.58, ...), kind=kOutput, calls=%fused_computation.38 | convolution fusion | flops 1628438528 | bytes 13008896 | tf_op jit(solution)/shard_map/jvp(hij,hjk->hik)/dot_general | solution.py:14
  72.8 4.7 fusion.21
  77.5 3.5 convolution_subtract_fusion.5
  81.0 5.1 fusion.19
  86.2 3.5 convolution_subtract_fusion.4
  89.7 4.9 fusion.17
  94.6 3.5 convolution_subtract_fusion.3
  98.1 4.7 fusion.15
  102.8 3.7 convolution_subtract_fusion.2
  106.5 4.7 fusion.13
  111.3 3.5 convolution_subtract_fusion.1
  114.8 5.1 fusion.11
  119.9 5.6 %convolution_subtract_fusion = f32[16,256,256]{1,2,0:T(8,128)} fusion(f32[16,256,256]{1,2,0:T(8,128)S(1)} %convolution_subtract_fusion.1, f32[16,256,256]{2,1,0:T(8,128)S(1)} %fusion.11), kind=kOutput, calls=%fused_computation.48 | convolution fusion | flops 1611661312 | bytes 12582912 | tf_op jit(solution)/shard_map/jvp(hij,hjk->hik)/dot_general | solution.py:14
  125.5 2.9 copy.348
  134.5 3.7 fusion.3
  138.2 2.9 fusion.75
  150.7 6.6 %all-to-all-start = ((f32[16,1,384,128]{3,2,1,0:T(8,128)}), f32[16,1,384,128]{3,2,1,0:T(8,128)}, u32[]{:S(2)}, u32[]{:S(2)}) async-start(f32[16,1,384,128]{3,2,1,0:T(8,128)} %maximum_bitcast_fusion), calls=%async_computation | async-start | bytes 6291456 | tf_op jit(solution)/shard_map/all_to_all | solution.py:130
  157.9 67.7 %all-to-all-done = f32[16,1,384,128]{3,2,1,0:T(8,128)} async-done(((f32[16,1,384,128]{3,2,1,0:T(8,128)}), f32[16,1,384,128]{3,2,1,0:T(8,128)}, u32[]{:S(2)}, u32[]{:S(2)}) %all-to-all-start) | async-done | bytes 3145760 | tf_op jit(solution)/shard_map/all_to_all | solution.py:130
  259.4 6.6 %all-to-all-start.1 = ((f32[16,1,256,128]{3,2,1,0:T(8,128)}), f32[16,1,256,128]{3,2,1,0:T(8,128)}, u32[]{:S(2)}, u32[]{:S(2)}) async-start(f32[16,1,256,128]{3,2,1,0:T(8,128)} %pad_maximum_fusion.2), calls=%async_computation.1 | async-start | bytes 4194304 | tf_op jit(solution)/shard_map/all_to_all | solution.py:149
  266.1 45.8 %all-to-all-done.1 = f32[16,1,256,128]{3,2,1,0:T(8,128)} async-done(((f32[16,1,256,128]{3,2,1,0:T(8,128)}), f32[16,1,256,128]{3,2,1,0:T(8,128)}, u32[]{:S(2)}, u32[]{:S(2)}) %all-to-all-start.1) | async-done | bytes 2097184 | tf_op jit(solution)/shard_map/all_to_all | solution.py:149
  311.9 4.3 fusion.89
  318.6 3.0 fusion.42
  324.2 5.0 fusion.35
  329.2 3.3 fusion.32
  332.5 4.3 fusion.30
  336.8 6.2 %fusion.36 = (f32[16,256]{1,0:T(8,128)}, f32[16,256]{1,0:T(8,128)S(1)}, f32[16,256]{1,0:T(8,128)S(1)}, f32[16,256,128]{2,1,0:T(8,128)}, f32[16,256,128]{2,1,0:T(8,128)S(1)}) fusion(f32[128,2,16,128]{3,0,1,2:T(8,128)S(1)} %copy-done.14, f32[16,256,256]{2,1,0:T(8,128)S(1)} %fusion.7, f32[16,2,128,128]{3,2,1,0:T(8,128)S(1)} %copy.316, ...), kind=kOutput, calls=%fused_computation.67 | convolution fusion | flops 406310912 | bytes 15794176 | tf_op jit(solution)/shard_map/transpose(jvp(hcv,hcd->hvd))/dot_general | solution.py:14
  344.6 3.7 fusion.146
  350.6 4.4 add_add_fusion.1
  355.0 3.0 copy.365
  358.0 2.9 fusion.38
  360.9 3.5 add_add_fusion
  364.4 3.1 copy.361
  370.0 4.2 fusion.106
  374.3 21.6 %multiply_reduce_fusion.3 = (f32[10240]{0:T(1024)S(1)}, f32[10240]{0:T(1024)S(1)}, f32[10240]{0:T(1024)S(1)}, f32[10240]{0:T(1024)S(1)}, f32[128,10240]{0,1:T(8,128)S(1)}) fusion(f32[131,10240]{0,1:T(8,128)} %copy-done, f32[128,10240]{0,1:T(8,128)} %get-tuple-element.70, f32[128,2048]{0,1:T(8,128)S(1)} %bitcast.500, f32[128,4096]{0,1:T(8,128)S(1)} %bitcast.496, ...), kind=kLoop, calls=%fused_computation.9 | loop fusion | flops 24862720 | bytes 36864000 | tf_op jit(solution)/shard_map/transpose(jvp())/reduce_sum | solution.py:71
  396.0 8.7 %broadcast_multiply_fusion = (f32[128,10240]{0,1:T(8,128)S(1)}, f32[128,10240]{0,1:T(8,128)S(1)}, f32[128,10240]{0,1:T(8,128)}, f32[128,10240]{0,1:T(8,128)}) fusion(f32[128,10240]{0,1:T(8,128)S(1)} %get-tuple-element.68, f32[10240]{0:T(1024)S(1)} %bitcast.510, f32[10240]{0:T(1024)S(1)} %bitcast.506, f32[10240]{0:T(1024)S(1)} %bitcast.508, ...), kind=kLoop, calls=%fused_computation.56 | loop fusion | flops 5242880 | bytes 26378240 | tf_op jit(solution)/shard_map/transpose(jvp())/mul | solution.py:71
  404.7 10.4 %pad_add_fusion = f32[131,10240]{0,1:T(8,128)S(1)} fusion(f32[128,10240]{0,1:T(8,128)S(1)} %get-tuple-element.72, f32[128,10240]{0,1:T(8,128)} %get-tuple-element.73, f32[128,10240]{0,1:T(8,128)} %get-tuple-element.74, f32[128,10240]{0,1:T(8,128)S(1)} %get-tuple-element.71), kind=kLoop, calls=%fused_computation | loop fusion | flops 4024320 | bytes 26337280 | tf_op jit(solution)/shard_map/transpose(jvp())/add_any | solution.py:69
  417.7 3.0 copy-done.2
  422.6 3.5 fusion.142
  433.6 3.9 copy.369
  439.9 4.6 fusion.110
  452.4 4.0 copy.370
  456.4 6.0 %slice_add_fusion = bf16[3,10240]{0,1:T(8,128)(2,1)} fusion(f32[3,10240]{0,1:T(8,128)} %copy.370, f32[131,10240]{0,1:T(8,128)} %copy-done.2), kind=kLoop, calls=%fused_computation.4 | loop fusion | flops 61440 | bytes 307200 | tf_op jit(solution)/shard_map/add | solution.py:178
  462.4 27.4 %scatter-add.4 = bf16[128,10240]{0,1:T(8,128)(2,1)S(1)} dynamic-update-slice(bf16[128,10240]{0,1:T(8,128)(2,1)S(1)} %copy-done.15, bf16[3,10240]{0,1:T(8,128)(2,1)} %slice_add_fusion, s32[]{:T(128)} %constant.321.clone.1, s32[]{:T(128)} %constant.304.clone.1) | dynamic-update-slice | bytes 122884 | tf_op jit(solution)/shard_map/scatter-add | solution.py:178
  496.9 21.2 %all-reduce.16.cloned.1.call-done = f32[4,10240]{1,0:T(4,128)} async-done(((f32[4,10240]{1,0:T(4,128)}), f32[4,10240]{1,0:T(4,128)}) %all-reduce.16.cloned.1.call-update) | async-done | bytes 163856 | tf_op jit(solution)/shard_map/psum | solution.py:179
  (271 shorter events, 120.8 us)
Async XLA Ops:
  7.2 4.6 copy-start.35
  12.8 9.0 %copy-start.69 = (f32[128,16]{0,1:T(8,128)S(1)}, f32[128,16]{0,1:T(8,128)}, u32[]{:S(2)}) copy-start(f32[128,16]{0,1:T(8,128)} %param.13) | copy-start | bytes 24580
  12.8 12.0 %copy-start.68 = (f32[128,32]{0,1:T(8,128)S(1)}, f32[128,32]{0,1:T(8,128)}, u32[]{:S(2)}) copy-start(f32[128,32]{0,1:T(8,128)} %param.12) | copy-start | bytes 49156
  12.8 13.9 %copy-start.19 = (bf16[128,2048]{1,0:T(8,128)(2,1)S(1)}, bf16[128,2048]{1,0:T(8,128)(2,1)}, u32[]{:S(2)}) copy-start(bf16[128,2048]{1,0:T(8,128)(2,1)} %param.15) | copy-start | bytes 1572868
  19.0 10.1 %collective-permute-start = (bf16[3,10240]{1,0:T(4,128)(2,1)}, bf16[3,10240]{1,0:T(4,128)(2,1)}, u32[]{:S(2)}, u32[]{:S(2)}) collective-permute-start(bf16[3,10240]{1,0:T(4,128)(2,1)} %copy.310), channel_id=1, source_target_pairs={{0,1},{1,2},{2,3},{3,4},{4,5},{5,6},{6,7},{7,8},{8,9},{9,10},{10,1... | collective-permute-start | bytes 184328 | tf_op jit(solution)/shard_map/ppermute | solution.py:20
  21.9 348.1 %copy-start.36 = (f32[16,128]{1,0:T(8,128)}, f32[16,128]{1,0:T(8,128)S(1)}, u32[]{:S(2)}) copy-start(f32[16,128]{1,0:T(8,128)S(1)} %fusion.162) | copy-start | bytes 24580
  24.7 13.2 %copy-start.37 = (f32[1,10240]{1,0:T(1,128)}, f32[1,10240]{1,0:T(1,128)S(1)}, u32[]{:S(2)}) copy-start(f32[1,10240]{1,0:T(1,128)S(1)} %get-tuple-element.82) | copy-start | bytes 122884
  24.7 13.2 %copy-start.39 = (f32[1,10240]{1,0:T(1,128)}, f32[1,10240]{1,0:T(1,128)S(1)}, u32[]{:S(2)}) copy-start(f32[1,10240]{1,0:T(1,128)S(1)} %get-tuple-element.83) | copy-start | bytes 122884
  24.7 13.2 %copy-start.41 = (f32[1,10240]{1,0:T(1,128)}, f32[1,10240]{1,0:T(1,128)S(1)}, u32[]{:S(2)}) copy-start(f32[1,10240]{1,0:T(1,128)S(1)} %get-tuple-element.84) | copy-start | bytes 122884
  24.7 13.2 %copy-start.43 = (f32[1,10240]{1,0:T(1,128)}, f32[1,10240]{1,0:T(1,128)S(1)}, u32[]{:S(2)}) copy-start(f32[1,10240]{1,0:T(1,128)S(1)} %get-tuple-element.85) | copy-start | bytes 122884
  27.7 342.3 %copy-start.33 = (pred[128,256]{1,0:T(8,128)(4,1)}, pred[128,256]{1,0:T(8,128)(4,1)S(1)}, u32[]{:S(2)}) copy-start(pred[128,256]{1,0:T(8,128)(4,1)S(1)} %broadcast_compare_fusion.1) | copy-start | bytes 98308
  37.9 11.9 %copy-start = (f32[131,10240]{0,1:T(8,128)}, f32[131,10240]{0,1:T(8,128)S(1)}, u32[]{:S(2)}) copy-start(f32[131,10240]{0,1:T(8,128)S(1)} %maximum_convert_fusion) | copy-start | bytes 16097284
  50.0 5.3 %copy-start.54 = (f32[128,2,16]{0,2,1:T(8,128)}, f32[128,2,16]{0,2,1:T(8,128)S(1)}, u32[]{:S(2)}) copy-start(f32[128,2,16]{0,2,1:T(8,128)S(1)} %multiply_reduce_fusion.7) | copy-start | bytes 49156
  59.3 55.4 %copy-start.22 = (f32[16,256,256]{1,2,0:T(8,128)}, f32[16,256,256]{1,2,0:T(8,128)S(1)}, u32[]{:S(2)}) copy-start(f32[16,256,256]{1,2,0:T(8,128)S(1)} %fusion.216) | copy-start | bytes 12582916
  65.8 7.0 %copy-start.65 = (pred[256,256]{0,1:T(8,128)(4,1)S(1)}, pred[256,256]{0,1:T(8,128)(4,1)}, u32[]{:S(2)}) copy-start(pred[256,256]{0,1:T(8,128)(4,1)} %get-tuple-element.97) | copy-start | bytes 196612
  131.5 12.2 %copy-start.8 = (f32[16,128,256]{2,1,0:T(8,128)}, f32[16,128,256]{2,1,0:T(8,128)S(1)}, u32[]{:S(2)}) copy-start(f32[16,128,256]{2,1,0:T(8,128)S(1)} %fusion.121) | copy-start | bytes 6291460
  138.2 8.1 %copy-start.5 = (f32[16,256,256]{2,1,0:T(8,128)}, f32[16,256,256]{2,1,0:T(8,128)S(1)}, u32[]{:S(2)}) copy-start(f32[16,256,256]{2,1,0:T(8,128)S(1)} %fusion.3) | copy-start | bytes 12582916
  138.2 5.5 %copy-start.20 = (bf16[128,2048]{1,0:T(8,128)(2,1)S(1)}, bf16[128,2048]{1,0:T(8,128)(2,1)}, u32[]{:S(2)}) copy-start(bf16[128,2048]{1,0:T(8,128)(2,1)} %param.15) | copy-start | bytes 1572868
  141.1 4.3 copy-start.25
  150.7 74.9 %all-to-all-start = ((f32[16,1,384,128]{3,2,1,0:T(8,128)}), f32[16,1,384,128]{3,2,1,0:T(8,128)}, u32[]{:S(2)}, u32[]{:S(2)}) async-start(f32[16,1,384,128]{3,2,1,0:T(8,128)} %maximum_bitcast_fusion), calls=%async_computation | async-start | bytes 6291456 | tf_op jit(solution)/shard_map/all_to_all | solution.py:130
  225.6 16.5 %copy-start.28 = (f32[16,1,128,128]{3,2,1,0:T(8,128)S(1)}, f32[16,1,128,128]{3,2,1,0:T(8,128)}, u32[]{:S(2)}) copy-start(f32[16,1,128,128]{3,2,1,0:T(8,128)} %constant_dynamic-update-slice_fusion.14) | copy-start | bytes 3145732
  257.9 8.1 %copy-start.45 = (f32[128,16]{1,0:T(8,128)S(1)}, f32[128,16]{1,0:T(8,128)}, u32[]{:S(2)}) copy-start(f32[128,16]{1,0:T(8,128)} %get-tuple-element.86) | copy-start | bytes 24580
  259.4 52.4 %all-to-all-start.1 = ((f32[16,1,256,128]{3,2,1,0:T(8,128)}), f32[16,1,256,128]{3,2,1,0:T(8,128)}, u32[]{:S(2)}, u32[]{:S(2)}) async-start(f32[16,1,256,128]{3,2,1,0:T(8,128)} %pad_maximum_fusion.2), calls=%async_computation.1 | async-start | bytes 4194304 | tf_op jit(solution)/shard_map/all_to_all | solution.py:149
  266.0 252.1 %all-reduce.16.cloned.1.call-start = ((), (), s32[]{:S(2)}) async-start(), calls=%async_computation.2 | async-start | bytes 327680 | tf_op jit(solution)/shard_map/psum | solution.py:179
  311.9 4.3 copy-start.6
  316.2 5.4 %copy-start.4 = (f32[16,256,256]{1,2,0:T(8,128)S(1)}, f32[16,256,256]{1,2,0:T(8,128)}, u32[]{:S(2)}) copy-start(f32[16,256,256]{1,2,0:T(8,128)} %convolution_subtract_fusion) | copy-start | bytes 12582916
  318.6 24.4 %copy-start.12 = (f32[16,256,128]{2,1,0:T(8,128)}, f32[16,256,128]{2,1,0:T(8,128)S(1)}, u32[]{:S(2)}) copy-start(f32[16,256,128]{2,1,0:T(8,128)S(1)} %slice_subtract_fusion) | copy-start | bytes 6291460
  332.4 4.4 copy-start.14
  336.8 6.2 %copy-start.9 = (f32[16,128,256]{2,1,0:T(8,128)S(1)}, f32[16,128,256]{2,1,0:T(8,128)}, u32[]{:S(2)}) copy-start(f32[16,128,256]{2,1,0:T(8,128)} %copy-done.8) | copy-start | bytes 6291460
  336.8 6.2 %copy-start.21 = (bf16[128,2048]{1,0:T(8,128)(2,1)S(1)}, bf16[128,2048]{1,0:T(8,128)(2,1)}, u32[]{:S(2)}) copy-start(bf16[128,2048]{1,0:T(8,128)(2,1)} %param.15) | copy-start | bytes 1572868
  343.0 84.6 %copy-start.56 = (f32[16,256]{1,0:T(8,128)}, f32[16,256]{1,0:T(8,128)S(1)}, u32[]{:S(2)}) copy-start(f32[16,256]{1,0:T(8,128)S(1)} %get-tuple-element.64) | copy-start | bytes 49156
  343.0 7.6 %copy-start.48 = (f32[16,256]{1,0:T(8,128)S(1)}, f32[16,256]{1,0:T(8,128)}, u32[]{:S(2)}) copy-start(f32[16,256]{1,0:T(8,128)} %copy.346) | copy-start | bytes 49156
  344.6 10.4 %copy-start.16 = (f32[16,256,128]{1,2,0:T(8,128)}, f32[16,256,128]{1,2,0:T(8,128)S(1)}, u32[]{:S(2)}) copy-start(f32[16,256,128]{1,2,0:T(8,128)S(1)} %get-tuple-element.129) | copy-start | bytes 6291460
  355.0 5.9 %copy-start.55 = (f32[128,2,16]{0,2,1:T(8,128)S(1)}, f32[128,2,16]{0,2,1:T(8,128)}, u32[]{:S(2)}) copy-start(f32[128,2,16]{0,2,1:T(8,128)} %copy-done.54) | copy-start | bytes 49156
  355.0 5.9 %copy-start.53 = (f32[128,2,16]{0,2,1:T(8,128)S(1)}, f32[128,2,16]{0,2,1:T(8,128)}, u32[]{:S(2)}) copy-start(f32[128,2,16]{0,2,1:T(8,128)} %copy-done.52) | copy-start | bytes 49156
  370.0 4.2 copy-start.18
  374.3 21.7 %copy-start.38 = (f32[1,10240]{1,0:T(1,128)S(1)}, f32[1,10240]{1,0:T(1,128)}, u32[]{:S(2)}) copy-start(f32[1,10240]{1,0:T(1,128)} %copy-done.37) | copy-start | bytes 122884
  374.3 21.7 %copy-start.40 = (f32[1,10240]{1,0:T(1,128)S(1)}, f32[1,10240]{1,0:T(1,128)}, u32[]{:S(2)}) copy-start(f32[1,10240]{1,0:T(1,128)} %copy-done.39) | copy-start | bytes 122884
  374.3 21.7 %copy-start.42 = (f32[1,10240]{1,0:T(1,128)S(1)}, f32[1,10240]{1,0:T(1,128)}, u32[]{:S(2)}) copy-start(f32[1,10240]{1,0:T(1,128)} %copy-done.41) | copy-start | bytes 122884
  374.3 21.7 %copy-start.44 = (f32[1,10240]{1,0:T(1,128)S(1)}, f32[1,10240]{1,0:T(1,128)}, u32[]{:S(2)}) copy-start(f32[1,10240]{1,0:T(1,128)} %copy-done.43) | copy-start | bytes 122884
  415.0 5.6 %copy-start.2 = (f32[131,10240]{0,1:T(8,128)}, f32[131,10240]{0,1:T(8,128)S(1)}, u32[]{:S(2)}) copy-start(f32[131,10240]{0,1:T(8,128)S(1)} %pad_add_fusion) | copy-start | bytes 16097284
  426.8 13.0 %copy-start.10 = (f32[16,128,256]{2,1,0:T(8,128)S(1)}, f32[16,128,256]{2,1,0:T(8,128)}, u32[]{:S(2)}) copy-start(f32[16,128,256]{2,1,0:T(8,128)} %copy-done.8) | copy-start | bytes 6291460
  432.2 7.7 %copy-start.24 = (f32[16,128,128]{1,2,0:T(8,128)S(1)}, f32[16,128,128]{1,2,0:T(8,128)}, u32[]{:S(2)}) copy-start(f32[16,128,128]{1,2,0:T(8,128)} %fusion.142) | copy-start | bytes 3145732
  437.6 9.0 %copy-start.27 = (f32[128,2,16]{2,0,1:T(8,128)S(1)}, f32[128,2,16]{2,0,1:T(8,128)}, u32[]{:S(2)}) copy-start(f32[128,2,16]{2,0,1:T(8,128)} %copy-done.26) | copy-start | bytes 49156
  437.6 9.0 %copy-start.30 = (f32[16,256]{0,1:T(8,128)S(1)}, f32[16,256]{0,1:T(8,128)}, u32[]{:S(2)}) copy-start(f32[16,256]{0,1:T(8,128)} %copy-done.29) | copy-start | bytes 49156
  437.6 9.0 %copy-start.32 = (f32[16,256]{0,1:T(8,128)S(1)}, f32[16,256]{0,1:T(8,128)}, u32[]{:S(2)}) copy-start(f32[16,256]{0,1:T(8,128)} %copy-done.31) | copy-start | bytes 49156
  437.6 14.9 %collective-permute-start.1 = (f32[3,10240]{1,0:T(4,128)}, f32[3,10240]{1,0:T(4,128)}, u32[]{:S(2)}, u32[]{:S(2)}) collective-permute-start(f32[3,10240]{1,0:T(4,128)} %copy.369), channel_id=1, source_target_pairs={{1,0},{2,1},{3,2},{4,3},{5,4},{6,5},{7,6},{8,7},{9,8},{10,9},{11,1... | collective-permute-start | bytes 368648 | tf_op jit(solution)/shard_map/ppermute | solution.py:20
  456.4 6.0 %copy-start.15 = (bf16[128,10240]{0,1:T(8,128)(2,1)S(1)}, bf16[128,10240]{0,1:T(8,128)(2,1)}, u32[]{:S(2)}) copy-start(bf16[128,10240]{0,1:T(8,128)(2,1)} %slice.417) | copy-start | bytes 7864324
  (28 other events, 79.8 us)
Sparse Core Ops, SparseCore 0:
  427.0 91.0 all-reduce.15

commit v2 on v1

--- a/solution.py
+++ b/solution.py
@@ -175,7 +175,7 @@
     _, table_cots = run_back((out_cot, carry_grad))
     grad_ext, grad_conv, grad_beta, grad_gate = prep_back(table_back(table_cots)[0])
     later_grads = shifted(grad_ext[:margin], "seq", -1)
-    grad_joined = grad_ext[margin:].at[tok_rows - margin :].add(later_grads)
+    grad_joined = grad_ext[margin:] + jnp.pad(later_grads, ((tok_rows - margin, 0), (0, 0)))
     conv_total = lax.psum(grad_conv, "seq")
     mixed = out.transpose(1, 0, 2).reshape(tok_rows, heads * DV)
     query_cols = query_raw.shape[1]

time: 536 us -> 510 us (0.951)
  local copies, waits for them, and re-layouts: 95.1 us -> 63.7 us
  waiting for transfers between devices: 135 us -> 142 us
    scatter-add x1 -> x0, local copies, waits for them, and re-layouts: 27.4 us -> none  [body(): grad_joined = grad_ext[margin:].at[tok_rows - margin:].add(later_grads)]
    psum x1, waiting for transfers between devices: 21.2 us -> 28.4 us  [body(): conv_total = lax.psum(grad_conv, 'seq')]
    another operation x1 -> x2, other arithmetic: 1.07 us -> 8.05 us
    add x1 -> x0, other arithmetic: 6.01 us -> none  [body(): grad_joined = grad_ext[margin:].at[tok_rows - margin:].add(later_grads)]
  transfers between devices with their start and end apart: 5 -> 5, of which waited for: 3 -> 3; matrix products, arithmetic and copies ran while one was open for 14% -> 13% of each run, Pallas kernels for 0% -> 0%
where the time goes in v2:
time: 510 us; the launch traced here: 501 us
  matrix products  167 us (33%)
  waiting for transfers between devices  142 us (28%)
  other arithmetic  95 us (19%)
  local copies, waits for them, and re-layouts  63.7 us (12%)
  starting transfers between devices  17.4 us (3%)
  between operations  16 us (3%)
    dot_general x64, matrix products, mm(): jnp.einsum(spec, a, b, precision=precision, preferred_element_type=jnp.fl...  160 us
    all_to_all x1, waiting for transfers between devices, spread(): return lax.all_to_all(x, axis, 0, 0)  67.7 us
    all_to_all x1, waiting for transfers between devices, chain(): both = lax.all_to_all(both, axis, 0, 0).reshape(heads * parts, 2 * rows, DK)  45.8 us
    psum x1, waiting for transfers between devices, body(): conv_total = lax.psum(grad_conv, 'seq')  28.4 us
    reduce_sum x1, other arithmetic, prepare_feats(): convolved = convolved + weights[offset] * extended[offset:offset + tok_rows]  22.4 us
    unnamed x165, local copies, waits for them, and re-layouts  21.2 us
    mul x1, other arithmetic, prepare_feats(): activated = jax.nn.silu(convolved)  11.9 us
  transfers between devices with their start and end apart: 5, of which 3 were waited for; matrix products, arithmetic and copies ran while one was open for 13% of the time, Pallas kernels for 0%

profile of v2, /device:TPU:8, one launch (start us, length us, event | category | flops | bytes accessed | tf_op | source)
XLA Modules:
  0.0 501.2 jit_solution(6575986285385903344)
XLA Ops:
  12.8 4.5 pad_maximum_fusion
  31.1 6.8 %maximum_convert_fusion = f32[131,10240]{0,1:T(8,128)S(1)} fusion(bf16[128,4096]{0,1:T(8,128)(2,1)} %copy.309, bf16[128,4096]{0,1:T(8,128)(2,1)} %copy.308, bf16[128,2048]{0,1:T(8,128)(2,1)} %copy.307, bf16[3,10240]{0,1:T(8,128)(2,1)S(1)} %copy.311), kind=kLoop, calls=%fused_computation.6 | loop fusion | flops 10731520 | bytes 8048640 | tf_op jit(solution)/shard_map/convert_element_type | solution.py:162
  38.0 11.9 %fusion.3 = (f32[128,10240]{0,1:T(8,128)S(1)}, f32[128,10240]{0,1:T(8,128)}) fusion(f32[131,10240]{0,1:T(8,128)S(1)} %maximum_convert_fusion, f32[10240]{0:T(1024)S(1)} %bitcast.509, f32[10240]{0:T(1024)S(1)} %bitcast.511, f32[10240]{0:T(1024)S(1)} %bitcast.507, f32[10240]{0:T(1024)S(1)} %bitcast.505), kind=kLoop, calls=%fused_computation.12 | loop fusion | flops 14417920 | bytes 31621120 | tf_op jit(solution)/shard_map/jvp(jit(silu))/mul | solution.py:72
  59.4 6.5 %fusion.24 = f32[16,256,256]{2,1,0:T(8,128)S(1)} fusion(f32[256,256]{0,1:T(8,128)S(1)} %copy-done.46, pred[256,256]{0,1:T(8,128)(4,1)S(1)} %copy-done.67, pred[256,256]{0,1:T(8,128)(4,1)S(1)} %copy-done.66, f32[16,256,256]{1,2,0:T(8,128)S(1)} %fusion.217, f32[16,256]{1,0:T(8,128)S(1)} %get-tuple-element.79, f32[16,256]{1,0:T(8,128)S(1)} %copy-done.49, ...), kind=kOutput, calls=%fused_computation.36 | convolution fusion | flops 1626341376 | bytes 8880128 | tf_op jit(solution)/shard_map/jvp(hij,hjk->hik)/dot_general | solution.py:14
  65.9 7.1 %fusion.26 = f32[16,256,256]{1,2,0:T(8,128)S(1)} fusion(f32[16,256,256]{2,1,0:T(8,128)S(1)} %fusion.24, f32[256,256]{0,1:T(8,128)S(1)} %copy-done.46, pred[256,256]{0,1:T(8,128)(4,1)S(1)} %copy-done.66, f32[16,256,256]{1,2,0:T(8,128)S(1)} %fusion.217, f32[16,256]{1,0:T(8,128)S(1)} %get-tuple-element.79, pred[256,256]{0,1:T(8,128)(4,1)S(1)} %copy-done.58, ...), kind=kOutput, calls=%fused_computation.39 | convolution fusion | flops 1628438528 | bytes 13008896 | tf_op jit(solution)/shard_map/jvp(hij,hjk->hik)/dot_general | solution.py:14
  73.0 4.7 fusion.22
  77.8 3.5 convolution_subtract_fusion.5
  81.3 4.9 fusion.20
  86.2 3.5 convolution_subtract_fusion.4
  89.7 4.9 fusion.18
  94.6 3.5 convolution_subtract_fusion.3
  98.1 4.7 fusion.16
  102.9 3.9 convolution_subtract_fusion.2
  106.8 4.7 fusion.14
  111.5 3.5 convolution_subtract_fusion.1
  115.0 4.9 fusion.12
  119.9 5.6 %convolution_subtract_fusion = f32[16,256,256]{1,2,0:T(8,128)} fusion(f32[16,256,256]{1,2,0:T(8,128)S(1)} %convolution_subtract_fusion.1, f32[16,256,256]{2,1,0:T(8,128)S(1)} %fusion.12), kind=kOutput, calls=%fused_computation.49 | convolution fusion | flops 1611661312 | bytes 12582912 | tf_op jit(solution)/shard_map/jvp(hij,hjk->hik)/dot_general | solution.py:14
  125.5 2.9 copy.348
  134.5 3.7 fusion.4
  138.3 2.9 fusion.76
  141.2 2.5 fusion.101
  150.8 6.6 %all-to-all-start = ((f32[16,1,384,128]{3,2,1,0:T(8,128)}), f32[16,1,384,128]{3,2,1,0:T(8,128)}, u32[]{:S(2)}, u32[]{:S(2)}) async-start(f32[16,1,384,128]{3,2,1,0:T(8,128)} %maximum_bitcast_fusion), calls=%async_computation | async-start | bytes 6291456 | tf_op jit(solution)/shard_map/all_to_all | solution.py:130
  158.0 67.7 %all-to-all-done = f32[16,1,384,128]{3,2,1,0:T(8,128)} async-done(((f32[16,1,384,128]{3,2,1,0:T(8,128)}), f32[16,1,384,128]{3,2,1,0:T(8,128)}, u32[]{:S(2)}, u32[]{:S(2)}) %all-to-all-start) | async-done | bytes 3145760 | tf_op jit(solution)/shard_map/all_to_all | solution.py:130
  259.5 6.6 %all-to-all-start.1 = ((f32[16,1,256,128]{3,2,1,0:T(8,128)}), f32[16,1,256,128]{3,2,1,0:T(8,128)}, u32[]{:S(2)}, u32[]{:S(2)}) async-start(f32[16,1,256,128]{3,2,1,0:T(8,128)} %pad_maximum_fusion.2), calls=%async_computation.1 | async-start | bytes 4194304 | tf_op jit(solution)/shard_map/all_to_all | solution.py:149
  266.1 45.8 %all-to-all-done.1 = f32[16,1,256,128]{3,2,1,0:T(8,128)} async-done(((f32[16,1,256,128]{3,2,1,0:T(8,128)}), f32[16,1,256,128]{3,2,1,0:T(8,128)}, u32[]{:S(2)}, u32[]{:S(2)}) %all-to-all-start.1) | async-done | bytes 2097184 | tf_op jit(solution)/shard_map/all_to_all | solution.py:149
  311.9 4.5 fusion.90
  318.8 3.0 fusion.43
  324.4 5.0 fusion.36
  329.4 3.0 fusion.33
  332.5 4.3 fusion.31
  336.8 6.2 %fusion.37 = (f32[16,256]{1,0:T(8,128)}, f32[16,256]{1,0:T(8,128)S(1)}, f32[16,256]{1,0:T(8,128)S(1)}, f32[16,256,128]{2,1,0:T(8,128)}, f32[16,256,128]{2,1,0:T(8,128)S(1)}) fusion(f32[128,2,16,128]{3,0,1,2:T(8,128)S(1)} %copy-done.14, f32[16,256,256]{2,1,0:T(8,128)S(1)} %fusion.8, f32[16,2,128,128]{3,2,1,0:T(8,128)S(1)} %copy.316, ...), kind=kOutput, calls=%fused_computation.68 | convolution fusion | flops 406310912 | bytes 15794176 | tf_op jit(solution)/shard_map/transpose(jvp(hcv,hcd->hvd))/dot_general | solution.py:14
  344.6 3.7 fusion.147
  350.6 3.5 fusion.143
  354.1 4.4 add_add_fusion.1
  358.5 3.0 copy.365
  361.5 2.9 fusion.39
  364.4 3.5 add_add_fusion
  367.9 3.1 copy.361
  373.6 4.2 fusion.107
  377.8 22.4 %multiply_reduce_fusion.3 = (f32[10240]{0:T(1024)S(1)}, f32[10240]{0:T(1024)S(1)}, f32[10240]{0:T(1024)S(1)}, f32[10240]{0:T(1024)S(1)}, f32[128,10240]{0,1:T(8,128)}) fusion(f32[131,10240]{0,1:T(8,128)} %copy-done, f32[128,10240]{0,1:T(8,128)} %get-tuple-element.58, f32[128,2048]{0,1:T(8,128)S(1)} %bitcast.500, f32[128,4096]{0,1:T(8,128)S(1)} %bitcast.496, ...), kind=kLoop, calls=%fused_computation.10 | loop fusion | flops 24862720 | bytes 36864000 | tf_op jit(solution)/shard_map/transpose(jvp())/reduce_sum | solution.py:71
  406.6 8.7 %broadcast_multiply_fusion = (f32[128,10240]{0,1:T(8,128)S(1)}, f32[128,10240]{0,1:T(8,128)S(1)}, f32[128,10240]{0,1:T(8,128)S(1)}, f32[128,10240]{0,1:T(8,128)S(1)}) fusion(f32[128,10240]{0,1:T(8,128)} %get-tuple-element.56, f32[10240]{0:T(1024)S(1)} %bitcast.510, f32[10240]{0:T(1024)S(1)} %bitcast.506, f32[10240]{0:T(1024)S(1)} %bitcast.508, ...), kind=kLoop, calls=%fused_computation.57 | loop fusion | flops 5242880 | bytes 26378240 | tf_op jit(solution)/shard_map/transpose(jvp())/mul | solution.py:71
  415.3 8.4 %pad_add_fusion = f32[131,10240]{0,1:T(8,128)S(1)} fusion(f32[128,10240]{0,1:T(8,128)S(1)} %get-tuple-element.60, f32[128,10240]{0,1:T(8,128)S(1)} %get-tuple-element.61, f32[128,10240]{0,1:T(8,128)S(1)} %get-tuple-element.62, f32[128,10240]{0,1:T(8,128)S(1)} %get-tuple-element.59), kind=kLoop, calls=%fused_computation | loop fusion | flops 4024320 | bytes 26337280 | tf_op jit(solution)/shard_map/transpose(jvp())/add_any | solution.py:69
  423.6 4.0 copy-done.2
  430.1 4.1 copy.369
  436.6 4.6 fusion.111
  449.1 4.0 copy.370
  453.1 7.0 %fusion.2 = bf16[128,10240]{0,1:T(8,128)(2,1)S(1)} fusion(f32[131,10240]{0,1:T(8,128)} %copy-done.2, f32[3,10240]{0,1:T(8,128)} %copy.370), kind=kLoop, calls=%fused_computation.5 | loop fusion | flops 2621440 | bytes 7987200 | tf_op jit(solution)/shard_map/convert.2
  463.9 28.4 %all-reduce.17.cloned.1.call-done = f32[4,10240]{1,0:T(4,128)} async-done(((f32[4,10240]{1,0:T(4,128)}), f32[4,10240]{1,0:T(4,128)}) %all-reduce.17.cloned.1.call-update) | async-done | bytes 163856 | tf_op jit(solution)/shard_map/psum | solution.py:179
  (269 shorter events, 111.8 us)
Async XLA Ops:
  7.2 4.6 copy-start.35
  12.8 9.0 %copy-start.69 = (f32[128,16]{0,1:T(8,128)S(1)}, f32[128,16]{0,1:T(8,128)}, u32[]{:S(2)}) copy-start(f32[128,16]{0,1:T(8,128)} %param.11) | copy-start | bytes 24580
  12.8 12.0 %copy-start.68 = (f32[128,32]{0,1:T(8,128)S(1)}, f32[128,32]{0,1:T(8,128)}, u32[]{:S(2)}) copy-start(f32[128,32]{0,1:T(8,128)} %param.10) | copy-start | bytes 49156
  12.8 13.9 %copy-start.18 = (bf16[128,2048]{1,0:T(8,128)(2,1)S(1)}, bf16[128,2048]{1,0:T(8,128)(2,1)}, u32[]{:S(2)}) copy-start(bf16[128,2048]{1,0:T(8,128)(2,1)} %param.13) | copy-start | bytes 1572868
  19.0 10.1 %collective-permute-start = (bf16[3,10240]{1,0:T(4,128)(2,1)}, bf16[3,10240]{1,0:T(4,128)(2,1)}, u32[]{:S(2)}, u32[]{:S(2)}) collective-permute-start(bf16[3,10240]{1,0:T(4,128)(2,1)} %copy.310), channel_id=1, source_target_pairs={{0,1},{1,2},{2,3},{3,4},{4,5},{5,6},{6,7},{7,8},{8,9},{9,10},{10,1... | collective-permute-start | bytes 184328 | tf_op jit(solution)/shard_map/ppermute | solution.py:20
  21.9 351.6 %copy-start.36 = (f32[16,128]{1,0:T(8,128)}, f32[16,128]{1,0:T(8,128)S(1)}, u32[]{:S(2)}) copy-start(f32[16,128]{1,0:T(8,128)S(1)} %fusion.163) | copy-start | bytes 24580
  24.7 13.2 %copy-start.37 = (f32[1,10240]{1,0:T(1,128)}, f32[1,10240]{1,0:T(1,128)S(1)}, u32[]{:S(2)}) copy-start(f32[1,10240]{1,0:T(1,128)S(1)} %get-tuple-element.70) | copy-start | bytes 122884
  24.7 13.2 %copy-start.39 = (f32[1,10240]{1,0:T(1,128)}, f32[1,10240]{1,0:T(1,128)S(1)}, u32[]{:S(2)}) copy-start(f32[1,10240]{1,0:T(1,128)S(1)} %get-tuple-element.71) | copy-start | bytes 122884
  24.7 13.2 %copy-start.41 = (f32[1,10240]{1,0:T(1,128)}, f32[1,10240]{1,0:T(1,128)S(1)}, u32[]{:S(2)}) copy-start(f32[1,10240]{1,0:T(1,128)S(1)} %get-tuple-element.72) | copy-start | bytes 122884
  24.7 13.2 %copy-start.43 = (f32[1,10240]{1,0:T(1,128)}, f32[1,10240]{1,0:T(1,128)S(1)}, u32[]{:S(2)}) copy-start(f32[1,10240]{1,0:T(1,128)S(1)} %get-tuple-element.73) | copy-start | bytes 122884
  27.7 345.9 %copy-start.33 = (pred[128,256]{1,0:T(8,128)(4,1)}, pred[128,256]{1,0:T(8,128)(4,1)S(1)}, u32[]{:S(2)}) copy-start(pred[128,256]{1,0:T(8,128)(4,1)S(1)} %broadcast_compare_fusion.1) | copy-start | bytes 98308
  37.9 11.9 %copy-start = (f32[131,10240]{0,1:T(8,128)}, f32[131,10240]{0,1:T(8,128)S(1)}, u32[]{:S(2)}) copy-start(f32[131,10240]{0,1:T(8,128)S(1)} %maximum_convert_fusion) | copy-start | bytes 16097284
  50.0 5.3 %copy-start.54 = (f32[128,2,16]{0,2,1:T(8,128)}, f32[128,2,16]{0,2,1:T(8,128)S(1)}, u32[]{:S(2)}) copy-start(f32[128,2,16]{0,2,1:T(8,128)S(1)} %multiply_reduce_fusion.7) | copy-start | bytes 49156
  59.4 55.7 %copy-start.21 = (f32[16,256,256]{1,2,0:T(8,128)}, f32[16,256,256]{1,2,0:T(8,128)S(1)}, u32[]{:S(2)}) copy-start(f32[16,256,256]{1,2,0:T(8,128)S(1)} %fusion.217) | copy-start | bytes 12582916
  65.9 7.2 %copy-start.65 = (pred[256,256]{0,1:T(8,128)(4,1)S(1)}, pred[256,256]{0,1:T(8,128)(4,1)}, u32[]{:S(2)}) copy-start(pred[256,256]{0,1:T(8,128)(4,1)} %get-tuple-element.85) | copy-start | bytes 196612
  131.6 12.2 %copy-start.8 = (f32[16,128,256]{2,1,0:T(8,128)}, f32[16,128,256]{2,1,0:T(8,128)S(1)}, u32[]{:S(2)}) copy-start(f32[16,128,256]{2,1,0:T(8,128)S(1)} %fusion.122) | copy-start | bytes 6291460
  138.2 8.2 %copy-start.5 = (f32[16,256,256]{2,1,0:T(8,128)}, f32[16,256,256]{2,1,0:T(8,128)S(1)}, u32[]{:S(2)}) copy-start(f32[16,256,256]{2,1,0:T(8,128)S(1)} %fusion.4) | copy-start | bytes 12582916
  138.2 5.5 %copy-start.19 = (bf16[128,2048]{1,0:T(8,128)(2,1)S(1)}, bf16[128,2048]{1,0:T(8,128)(2,1)}, u32[]{:S(2)}) copy-start(bf16[128,2048]{1,0:T(8,128)(2,1)} %param.13) | copy-start | bytes 1572868
  141.2 4.3 copy-start.25
  150.8 74.9 %all-to-all-start = ((f32[16,1,384,128]{3,2,1,0:T(8,128)}), f32[16,1,384,128]{3,2,1,0:T(8,128)}, u32[]{:S(2)}, u32[]{:S(2)}) async-start(f32[16,1,384,128]{3,2,1,0:T(8,128)} %maximum_bitcast_fusion), calls=%async_computation | async-start | bytes 6291456 | tf_op jit(solution)/shard_map/all_to_all | solution.py:130
  225.7 16.5 %copy-start.28 = (f32[16,1,128,128]{3,2,1,0:T(8,128)S(1)}, f32[16,1,128,128]{3,2,1,0:T(8,128)}, u32[]{:S(2)}) copy-start(f32[16,1,128,128]{3,2,1,0:T(8,128)} %constant_dynamic-update-slice_fusion.14) | copy-start | bytes 3145732
  257.9 8.1 %copy-start.45 = (f32[128,16]{1,0:T(8,128)S(1)}, f32[128,16]{1,0:T(8,128)}, u32[]{:S(2)}) copy-start(f32[128,16]{1,0:T(8,128)} %get-tuple-element.74) | copy-start | bytes 24580
  259.5 52.4 %all-to-all-start.1 = ((f32[16,1,256,128]{3,2,1,0:T(8,128)}), f32[16,1,256,128]{3,2,1,0:T(8,128)}, u32[]{:S(2)}, u32[]{:S(2)}) async-start(f32[16,1,256,128]{3,2,1,0:T(8,128)} %pad_maximum_fusion.2), calls=%async_computation.1 | async-start | bytes 4194304 | tf_op jit(solution)/shard_map/all_to_all | solution.py:149
  266.0 226.3 %all-reduce.17.cloned.1.call-start = ((), (), s32[]{:S(2)}) async-start(), calls=%async_computation.2 | async-start | bytes 327680 | tf_op jit(solution)/shard_map/psum | solution.py:179
  311.9 4.5 copy-start.6
  316.4 5.4 %copy-start.4 = (f32[16,256,256]{1,2,0:T(8,128)S(1)}, f32[16,256,256]{1,2,0:T(8,128)}, u32[]{:S(2)}) copy-start(f32[16,256,256]{1,2,0:T(8,128)} %convolution_subtract_fusion) | copy-start | bytes 12582916
  318.8 24.2 %copy-start.12 = (f32[16,256,128]{2,1,0:T(8,128)}, f32[16,256,128]{2,1,0:T(8,128)S(1)}, u32[]{:S(2)}) copy-start(f32[16,256,128]{2,1,0:T(8,128)S(1)} %slice_subtract_fusion) | copy-start | bytes 6291460
  332.5 4.4 copy-start.14
  336.8 6.2 %copy-start.9 = (f32[16,128,256]{2,1,0:T(8,128)S(1)}, f32[16,128,256]{2,1,0:T(8,128)}, u32[]{:S(2)}) copy-start(f32[16,128,256]{2,1,0:T(8,128)} %copy-done.8) | copy-start | bytes 6291460
  336.8 6.2 %copy-start.20 = (bf16[128,2048]{1,0:T(8,128)(2,1)S(1)}, bf16[128,2048]{1,0:T(8,128)(2,1)}, u32[]{:S(2)}) copy-start(bf16[128,2048]{1,0:T(8,128)(2,1)} %param.13) | copy-start | bytes 1572868
  343.0 58.8 %copy-start.56 = (f32[16,256]{1,0:T(8,128)}, f32[16,256]{1,0:T(8,128)S(1)}, u32[]{:S(2)}) copy-start(f32[16,256]{1,0:T(8,128)S(1)} %get-tuple-element.52) | copy-start | bytes 49156
  344.6 13.9 %copy-start.15 = (f32[16,256,128]{1,2,0:T(8,128)}, f32[16,256,128]{1,2,0:T(8,128)S(1)}, u32[]{:S(2)}) copy-start(f32[16,256,128]{1,2,0:T(8,128)S(1)} %get-tuple-element.117) | copy-start | bytes 6291460
  344.6 9.4 %copy-start.48 = (f32[16,256]{1,0:T(8,128)S(1)}, f32[16,256]{1,0:T(8,128)}, u32[]{:S(2)}) copy-start(f32[16,256]{1,0:T(8,128)} %copy.346) | copy-start | bytes 49156
  358.5 5.9 %copy-start.55 = (f32[128,2,16]{0,2,1:T(8,128)S(1)}, f32[128,2,16]{0,2,1:T(8,128)}, u32[]{:S(2)}) copy-start(f32[128,2,16]{0,2,1:T(8,128)} %copy-done.54) | copy-start | bytes 49156
  358.5 5.9 %copy-start.53 = (f32[128,2,16]{0,2,1:T(8,128)S(1)}, f32[128,2,16]{0,2,1:T(8,128)}, u32[]{:S(2)}) copy-start(f32[128,2,16]{0,2,1:T(8,128)} %copy-done.52) | copy-start | bytes 49156
  373.5 4.2 copy-start.16
  373.6 4.2 copy-start.17
  377.8 27.0 %copy-start.24 = (f32[16,128,128]{1,2,0:T(8,128)S(1)}, f32[16,128,128]{1,2,0:T(8,128)}, u32[]{:S(2)}) copy-start(f32[16,128,128]{1,2,0:T(8,128)} %copy.374) | copy-start | bytes 3145732
  377.8 28.8 %copy-start.38 = (f32[1,10240]{1,0:T(1,128)S(1)}, f32[1,10240]{1,0:T(1,128)}, u32[]{:S(2)}) copy-start(f32[1,10240]{1,0:T(1,128)} %copy-done.37) | copy-start | bytes 122884
  377.8 28.8 %copy-start.40 = (f32[1,10240]{1,0:T(1,128)S(1)}, f32[1,10240]{1,0:T(1,128)}, u32[]{:S(2)}) copy-start(f32[1,10240]{1,0:T(1,128)} %copy-done.39) | copy-start | bytes 122884
  377.8 28.8 %copy-start.42 = (f32[1,10240]{1,0:T(1,128)S(1)}, f32[1,10240]{1,0:T(1,128)}, u32[]{:S(2)}) copy-start(f32[1,10240]{1,0:T(1,128)} %copy-done.41) | copy-start | bytes 122884
  377.8 28.8 %copy-start.44 = (f32[1,10240]{1,0:T(1,128)S(1)}, f32[1,10240]{1,0:T(1,128)}, u32[]{:S(2)}) copy-start(f32[1,10240]{1,0:T(1,128)} %copy-done.43) | copy-start | bytes 122884
  430.1 6.4 %copy-start.10 = (f32[16,128,256]{2,1,0:T(8,128)S(1)}, f32[16,128,256]{2,1,0:T(8,128)}, u32[]{:S(2)}) copy-start(f32[16,128,256]{2,1,0:T(8,128)} %copy-done.8) | copy-start | bytes 6291460
  430.1 6.4 %copy-start.23 = (f32[16,128,128]{1,2,0:T(8,128)S(1)}, f32[16,128,128]{1,2,0:T(8,128)}, u32[]{:S(2)}) copy-start(f32[16,128,128]{1,2,0:T(8,128)} %fusion.143) | copy-start | bytes 3145732
  434.2 9.0 %copy-start.27 = (f32[128,2,16]{2,0,1:T(8,128)S(1)}, f32[128,2,16]{2,0,1:T(8,128)}, u32[]{:S(2)}) copy-start(f32[128,2,16]{2,0,1:T(8,128)} %copy-done.26) | copy-start | bytes 49156
  434.2 9.0 %copy-start.30 = (f32[16,256]{0,1:T(8,128)S(1)}, f32[16,256]{0,1:T(8,128)}, u32[]{:S(2)}) copy-start(f32[16,256]{0,1:T(8,128)} %copy-done.29) | copy-start | bytes 49156
  434.2 9.0 %copy-start.32 = (f32[16,256]{0,1:T(8,128)S(1)}, f32[16,256]{0,1:T(8,128)}, u32[]{:S(2)}) copy-start(f32[16,256]{0,1:T(8,128)} %copy-done.31) | copy-start | bytes 49156
  434.2 14.9 %collective-permute-start.1 = (f32[3,10240]{1,0:T(4,128)}, f32[3,10240]{1,0:T(4,128)}, u32[]{:S(2)}, u32[]{:S(2)}) collective-permute-start(f32[3,10240]{1,0:T(4,128)} %copy.369), channel_id=1, source_target_pairs={{1,0},{2,1},{3,2},{4,3},{5,4},{6,5},{7,6},{8,7},{9,8},{10,9},{11,1... | collective-permute-start | bytes 368648 | tf_op jit(solution)/shard_map/ppermute | solution.py:20
  (28 other events, 79.8 us)
Sparse Core Ops, SparseCore 0:
  401.2 91.1 all-reduce.16
